TPU v7x, 32 devices: a whole 2x2x4 slice. The times are simulated.
32 devices in a mesh: space: 4 (over z), chaos: 8 (over y, x, core).
Axes of the slice: x: 2, y: 2, z: 4, core: 2. Of those that a mesh axis runs over, the one named last changes fastest.
Arguments:
- velocity: float32 [40, 3, 4, 64, 128], P('chaos', None, 'space')
- base_velocity: float32 [40, 3, 4, 64, 128], P('chaos', None, 'space')
- mode_slot: int32 [35], replicated, may hold values from 0 to 39, as said below
- triples: int32 [4096, 3], replicated, may hold values from 0 to 34, as said below
- triple_coef: bfloat16 [4096], replicated, may hold values from -0.29882812 to 0.29882812
Outputs:
- convection: float32 [40, 3, 4, 64, 128], P('chaos', None, 'space')
- next_velocity: float32 [40, 3, 4, 64, 128], P('chaos', None, 'space')
Inputs may be any that keep to these rules, and one draw needn't show every extreme that they name: `mode_slot`: the modes take distinct slots; slots that hold no mode are zero in velocity and base_velocity. `triples`: each triple (i, j, k) of modes is listed at most once.
All inputs are finite; a program needn't handle non-finite values.
Results may differ from a plain program's by a relative error of at most 0.0052.
Values may be sent and summed in bfloat16 or wider, within the bound.
No kernel may reach another device: no remote copies, remote signals or barrier semaphores. Data moves between devices by JAX's collectives and lax.ppermute only.
A program may use at most 192 MiB of HBM per device.

v0:
```python
import functools

import jax
import jax.numpy as jnp
import numpy as np
from jax import lax
from jax.experimental import pallas as pl
from jax.experimental.pallas import tpu as pltpu
from jax.sharding import PartitionSpec as P

SECTION_STEP = 0.5
COMPS = 3
LANES = 128
LANE_BITS = 7
TILE = 256
PACK = 16
VMEM_LIMIT = 48 * 1024 * 1024


def round_up(value, unit):
    return -(-value // unit) * unit


def vmem_spec():
    return pl.BlockSpec(memory_space=pltpu.VMEM)


def params():
    return pltpu.CompilerParams(vmem_limit_bytes=VMEM_LIMIT)


class Plan:
    def __init__(self, slot_dev, ny, nz, planes, chunks, modes):
        self.slot_dev, self.ny, self.planes, self.chunks, self.modes = slot_dev, ny, planes, chunks, modes
        self.fields = slot_dev * COMPS
        self.packed = round_up(self.fields, 16)
        self.wide = chunks * self.packed
        self.rows = ny // chunks
        self.width = nz // planes
        assert nz == LANES and self.width * planes == nz and self.rows * chunks == ny
        self.width_bits = self.width.bit_length() - 1
        assert self.rest_fits(modes)
        assert planes & (planes - 1) == 0 and 2 * self.rows <= self.width
        self.inner = -(-self.rows // planes)
        if self.rows % planes == 0:
            assert planes >= 3
            self.vectors = self.inner + 1
            first = self.inner * planes
            self.low, self.high, self.side = first, first + 1, first + 2
        else:
            assert self.rows + 3 <= planes
            self.vectors = 1
            self.low, self.high, self.side = planes - 1, self.rows, self.rows + 1
        self.mode_pad = round_up(modes, 8)
        self.main = modes // 16 * 16
        self.rest = modes - self.main
        self.wide_pad = round_up(modes, PACK)
        self.rest_rows = self.rest * self.wide_pad
        self.pairs = modes * self.main
        self.depth = round_up(self.pairs + self.rest_rows, TILE)
        self.groups = self.depth // TILE
        self.lanes = self.inner * COMPS * LANES
        self.cuts = [(at, min(at + TILE, self.lanes)) for at in range(0, self.lanes, TILE)]

    @staticmethod
    def rest_fits(modes):
        return modes >= PACK and modes % PACK <= 8

    def stencil(self):
        out = np.zeros((self.vectors * LANES, 2 * self.inner * LANES), np.float32)
        width = self.width
        for r in range(self.rows):
            above = r + 1 if r + 1 < self.rows else self.high
            below = r - 1 if r > 0 else self.low
            for w in range(width):
                at = r * width + w
                out[above * width + w, at] += 0.5
                out[below * width + w, at] -= 0.5
                right = at + 1 if w + 1 < width else self.side * width + 2 * r + 1
                left = at - 1 if w > 0 else self.side * width + 2 * r
                out[right, self.inner * LANES + at] += 0.5
                out[left, self.inner * LANES + at] -= 0.5
        return out


def block_transposer(plan):
    size = plan.planes * LANES
    source = lax.broadcasted_iota(jnp.int32, (size, size), 0)
    target = lax.broadcasted_iota(jnp.int32, (size, size), 1)
    part, lane = source >> LANE_BITS, source & (LANES - 1)
    block, inner = lane >> plan.width_bits, lane & (plan.width - 1)
    wanted = (block << LANE_BITS) + (part << plan.width_bits) + inner
    return jnp.where(target == wanted, 1.0, 0.0).astype(jnp.bfloat16)


def side_collector(plan):
    source = lax.broadcasted_iota(jnp.int32, (plan.rows * LANES, LANES), 0)
    target = lax.broadcasted_iota(jnp.int32, (plan.rows * LANES, LANES), 1)
    block, inner = target >> plan.width_bits, target & (plan.width - 1)
    beside = (block << plan.width_bits) - 1 + (inner & 1) * (plan.width + 1)
    wanted = ((inner >> 1) << LANE_BITS) + (beside & (LANES - 1))
    return jnp.where((source == wanted) & (inner < 2 * plan.rows), 1.0, 0.0).astype(jnp.bfloat16)


def pack_kernel(plan, v_ref, out_ref):
    planes, rows, chunks, packed = plan.planes, plan.rows, plan.chunks, plan.packed
    pad = jnp.zeros((packed - plan.fields, LANES), jnp.float32)
    lines = []
    for y in range(plan.ny):
        block = v_ref[pl.ds(y, plan.fields, stride=plan.ny), :]
        lines.append(jnp.concatenate([block, pad], axis=0).astype(jnp.bfloat16))

    def across(offset):
        return jnp.concatenate([lines[(c * rows + offset) % plan.ny] for c in range(chunks)], axis=0)

    transposer = block_transposer(plan)
    inside = [across(r) for r in range(rows)]
    side = jnp.dot(jnp.concatenate(inside, axis=1), side_collector(plan), preferred_element_type=jnp.float32)
    blocks = inside + [jnp.zeros_like(inside[0])] * (plan.vectors * planes - rows)
    blocks[plan.low] = across(-1)
    blocks[plan.high] = across(rows)
    blocks[plan.side] = side.astype(jnp.bfloat16)
    for v in range(plan.vectors):
        row = jnp.concatenate(blocks[v * planes : (v + 1) * planes], axis=1)
        swapped = jnp.dot(row, transposer, preferred_element_type=jnp.float32).astype(jnp.bfloat16)
        for s in range(planes):
            for c in range(chunks):
                out_ref[s, c, v] = swapped[c * packed : (c + 1) * packed, s * LANES : (s + 1) * LANES]


def prepare_kernel(plan, slot_ref, triples_ref, coef_ref, table_ref, pick_ref, place_ref, swap_ref):
    count = triples_ref.shape[1]
    mode_i = triples_ref[0:1, :]
    mode_j = triples_ref[1:2, :]
    mode_k = triples_ref[2:3, :]
    place = jnp.where(
        mode_j < plan.main,
        mode_i * plan.main + mode_j,
        plan.pairs + (mode_j - plan.main) * plan.wide_pad + mode_i,
    )
    row = (place // TILE) * plan.mode_pad + mode_k
    column = place % TILE
    coef = coef_ref[...].astype(jnp.float32)
    height = plan.groups * plan.mode_pad
    total = jnp.zeros((height, TILE), jnp.float32)
    step = 1024 if count % 1024 == 0 else count
    row_iota = lax.broadcasted_iota(jnp.int32, (height, step), 0)
    column_iota = lax.broadcasted_iota(jnp.int32, (TILE, step), 0)
    for start in range(0, count, step):
        part = slice(start, start + step)
        left = jnp.where(row_iota == row[:, part], coef[:, part], 0.0).astype(jnp.bfloat16)
        right = jnp.where(column_iota == column[:, part], 1.0, 0.0).astype(jnp.bfloat16)
        total = total + lax.dot_general(
            left, right, (((1,), (1,)), ((), ())), preferred_element_type=jnp.float32
        )
    for g in range(plan.groups):
        table_ref[:, g * TILE : (g + 1) * TILE] = total[g * plan.mode_pad : (g + 1) * plan.mode_pad].astype(jnp.bfloat16)

    shape = (plan.wide_pad, plan.wide)
    column = lax.broadcasted_iota(jnp.int32, shape, 1)
    mode = lax.broadcasted_iota(jnp.int32, shape, 0)
    inner = column % plan.packed
    slot = jnp.where(
        inner < plan.fields, (column // plan.packed) * plan.slot_dev + inner // COMPS, -1
    )
    wanted = jnp.full(shape, -2, jnp.int32)
    for m in range(plan.modes):
        wanted = jnp.where(mode == m, slot_ref[m], wanted)
    hit = jnp.where(wanted == slot, 1.0, 0.0)
    pickers = [jnp.where(inner % COMPS == d, hit, 0.0) for d in range(COMPS)]
    pick_ref[...] = jnp.concatenate(pickers, axis=0).astype(jnp.bfloat16)
    narrow = jnp.concatenate([picker[: plan.mode_pad] for picker in pickers], axis=0)
    place_ref[...] = narrow.T.astype(jnp.bfloat16)
    swap_ref[...] = block_transposer(plan)


def contract_kernel(plan, got_ref, stencil_ref, table_ref, pick_ref, place_ref, out_ref, *scratch):
    moving_ref, row_ref, slope_ref, conv_ref, even_ref, odd_ref = scratch
    planes, inner, pad, main, wide = plan.planes, plan.inner, plan.mode_pad, plan.main, plan.wide_pad
    tail = plan.pairs + plan.rest_rows
    if tail < plan.depth:
        for ref in (even_ref, odd_ref):
            ref[tail:, :] = jnp.zeros((plan.depth - tail, ref.shape[1]), jnp.bfloat16)

    def vector(p, v):
        return got_ref[p % planes, :, v].reshape(plan.wide, LANES)

    for p in range(planes):
        center = jnp.concatenate([vector(p, v) for v in range(plan.vectors)], axis=1)
        along_x = [
            (0.5 * (vector(p + 1, v).astype(jnp.float32) - vector(p - 1, v).astype(jnp.float32))).astype(jnp.bfloat16)
            for v in range(inner)
        ]
        along_yz = jnp.dot(center, stencil_ref[...], preferred_element_type=jnp.float32).astype(jnp.bfloat16)
        moving = center[:, : inner * LANES]
        moving_ref[p] = jnp.dot(pick_ref[...], moving, preferred_element_type=jnp.float32)
        slopes = jnp.dot(
            pick_ref[...], jnp.concatenate(along_x + [along_yz], axis=1), preferred_element_type=jnp.float32
        )
        slope_ref[p] = slopes.astype(jnp.bfloat16)
        for c in range(COMPS):
            row_ref[p, c * 8 : (c + 1) * 8] = slopes[c * wide + main : c * wide + main + 8]

    def repeated(row):
        return jnp.broadcast_to(row, (PACK, LANES)).astype(jnp.bfloat16)

    def along(left, right):
        term = left[0] * right[0]
        for d in range(1, COMPS):
            term = term + left[d] * right[d]
        return term

    def fill(prod_ref, p, v):
        here = slice(v * LANES, (v + 1) * LANES)

        def there(d):
            return slice((d * inner + v) * LANES, (d * inner + v + 1) * LANES)

        def lanes(c):
            return slice((v * COMPS + c) * LANES, (v * COMPS + c + 1) * LANES)

        slopes = {
            (c, j): [slope_ref[p, c * wide + j : c * wide + j + PACK, there(d)] for d in range(COMPS)]
            for c in range(COMPS)
            for j in range(0, main, PACK)
        }
        for i in range(plan.modes):
            moving = [repeated(moving_ref[p, d * wide + i : d * wide + i + 1, here]) for d in range(COMPS)]
            for c in range(COMPS):
                for j in range(0, main, PACK):
                    prod_ref[i * main + j : i * main + j + PACK, lanes(c)] = along(moving, slopes[c, j])
        if plan.rest:
            moving = {
                i: [moving_ref[p, d * wide + i : d * wide + i + PACK, here].astype(jnp.bfloat16) for d in range(COMPS)]
                for i in range(0, wide, PACK)
            }
            for c in range(COMPS):
                for j in range(plan.rest):
                    slope = [repeated(row_ref[p, c * 8 + j : c * 8 + j + 1, there(d)]) for d in range(COMPS)]
                    for i in range(0, wide, PACK):
                        at = plan.pairs + j * wide + i
                        prod_ref[at : at + PACK, lanes(c)] = along(moving[i], slope)

    def multiply(slot, prod_ref, cut):
        low, high = cut
        result = jnp.dot(table_ref[...], prod_ref[:, low:high], preferred_element_type=jnp.float32)
        for at in range(low, high, LANES):
            v, c = divmod(at // LANES, COMPS)
            conv_ref[slot, v, c * pad : (c + 1) * pad, :] = result[:, at - low : at - low + LANES]

    def beside(prod_ref, p, done_ref, slot):
        cuts = list(plan.cuts)
        for v in range(inner):
            if cuts:
                multiply(slot, done_ref, cuts.pop(0))
            fill(prod_ref, p, v)
        for cut in cuts:
            multiply(slot, done_ref, cut)

    def two_planes(step, carry):
        p = 2 * step
        beside(even_ref, p, odd_ref, p)
        beside(odd_ref, p + 1, even_ref, p + 1)
        return carry

    lax.fori_loop(0, planes // 2, two_planes, 0)
    for cut in plan.cuts:
        multiply(planes, odd_ref, cut)
    for p in range(planes):
        stacked = jnp.concatenate([conv_ref[p + 1, v].astype(jnp.bfloat16) for v in range(inner)], axis=1)
        placed = jnp.dot(place_ref[...], stacked, preferred_element_type=jnp.float32).astype(jnp.bfloat16)
        for v in range(inner):
            block = placed[:, v * LANES : (v + 1) * LANES]
            out_ref[p, :, v] = block.reshape(plan.chunks, plan.packed, LANES)


def finish_kernel(plan, got_ref, base_ref, swap_ref, conv_ref, next_ref, flat_ref, conv_vmem, next_vmem, sems):
    for v in range(plan.inner):
        parts = [got_ref[s, :, v].reshape(plan.wide, LANES) for s in range(plan.planes)]
        swapped = jnp.dot(jnp.concatenate(parts, axis=1), swap_ref[...], preferred_element_type=jnp.float32)
        for block in range(min(plan.planes, plan.rows - v * plan.planes)):
            for chunk in range(plan.chunks):
                at = (chunk * plan.rows + v * plan.planes + block) * plan.packed
                flat_ref[at : at + plan.packed, :] = swapped[
                    chunk * plan.packed : (chunk + 1) * plan.packed, block * LANES : (block + 1) * LANES
                ]
    copies = []
    for s in range(plan.slot_dev):
        fields = slice(s * COMPS, (s + 1) * COMPS)
        for f in range(s * COMPS, (s + 1) * COMPS):
            value = flat_ref[pl.ds(f, plan.ny, stride=plan.packed), :]
            conv_vmem[f] = value
            next_vmem[f] = base_ref[f] - SECTION_STEP * value
        for which, (source, target) in enumerate(((conv_vmem, conv_ref), (next_vmem, next_ref))):
            copies.append(pltpu.make_async_copy(source.at[fields], target.at[fields], sems.at[which, s]))
            copies[-1].start()
    for copy in copies:
        copy.wait()


def on_device(velocity, base_velocity, mode_slot, triples, triple_coef):
    slot_dev, _, _, ny, nz = velocity.shape
    chunks, planes = lax.axis_size("chaos"), lax.axis_size("space")
    plan = Plan(slot_dev, ny, nz, planes, chunks, mode_slot.shape[0])
    fields, packed, devices = plan.fields, plan.packed, planes * chunks

    def exchange(block):
        flat = block.reshape((devices,) + block.shape[2:])
        return lax.all_to_all(flat, ("space", "chaos"), 0, 0, tiled=True).reshape(block.shape)

    sent = pl.pallas_call(
        functools.partial(pack_kernel, plan),
        out_shape=jax.ShapeDtypeStruct((planes, chunks, plan.vectors, packed, LANES), jnp.bfloat16),
        in_specs=[vmem_spec()],
        out_specs=vmem_spec(),
        compiler_params=params(),
        name="pack",
    )(velocity.reshape(fields * ny, nz))
    got = exchange(sent)
    table, pick, place, swap = pl.pallas_call(
        functools.partial(prepare_kernel, plan),
        out_shape=[
            jax.ShapeDtypeStruct((plan.mode_pad, plan.depth), jnp.bfloat16),
            jax.ShapeDtypeStruct((COMPS * plan.wide_pad, plan.wide), jnp.bfloat16),
            jax.ShapeDtypeStruct((plan.wide, COMPS * plan.mode_pad), jnp.bfloat16),
            jax.ShapeDtypeStruct((planes * LANES, planes * LANES), jnp.bfloat16),
        ],
        in_specs=[pl.BlockSpec(memory_space=pltpu.SMEM)] + [vmem_spec()] * 2,
        out_specs=[vmem_spec()] * 4,
        compiler_params=params(),
        name="prepare",
    )(mode_slot, triples.T, triple_coef.reshape(1, -1))
    returned = pl.pallas_call(
        functools.partial(contract_kernel, plan),
        out_shape=jax.ShapeDtypeStruct((planes, chunks, plan.inner, packed, LANES), jnp.bfloat16),
        in_specs=[vmem_spec()] * 5,
        out_specs=vmem_spec(),
        scratch_shapes=[
            pltpu.VMEM((planes, COMPS * plan.wide_pad, plan.inner * LANES), jnp.float32),
            pltpu.VMEM((planes, COMPS * 8, plan.lanes), jnp.float32),
            pltpu.VMEM((planes, COMPS * plan.wide_pad, plan.lanes), jnp.bfloat16),
            pltpu.VMEM((planes + 1, plan.inner, COMPS * plan.mode_pad, LANES), jnp.float32),
            pltpu.VMEM((plan.depth, plan.lanes), jnp.bfloat16),
            pltpu.VMEM((plan.depth, plan.lanes), jnp.bfloat16),
        ],
        compiler_params=params(),
        name="contract",
    )(got, jnp.asarray(plan.stencil(), jnp.bfloat16), table, pick, place)
    convection, next_velocity = pl.pallas_call(
        functools.partial(finish_kernel, plan),
        out_shape=[jax.ShapeDtypeStruct((fields, ny, nz), jnp.float32)] * 2,
        in_specs=[vmem_spec()] * 3,
        out_specs=[pl.BlockSpec(memory_space=pl.ANY)] * 2,
        scratch_shapes=[
            pltpu.VMEM((ny * packed, LANES), jnp.float32),
            pltpu.VMEM((fields, ny, nz), jnp.float32),
            pltpu.VMEM((fields, ny, nz), jnp.float32),
            pltpu.SemaphoreType.DMA((2, slot_dev)),
        ],
        compiler_params=params(),
        name="finish",
    )(exchange(returned), base_velocity.reshape(fields, ny, nz), swap)
    return convection.reshape(velocity.shape), next_velocity.reshape(velocity.shape)


def solution(mesh):
    spread = P("chaos", None, "space", None, None)
    return jax.shard_map(
        on_device,
        mesh=mesh,
        in_specs=(spread, spread, P(), P(), P()),
        out_specs=(spread, spread),
        check_vma=False,
    )
```

profile of v0, /device:TPU:0, one launch (start us, length us, event | category | flops | bytes accessed | tf_op | source)
XLA Modules:
  0.0 43.2 jit_solution(2766461421271788896)
XLA Ops:
  0.6 0.0 copy-start
  0.6 1.0 %copy-done = f32[5,3,1,64,128]{4,3,2,1,0:T(8,128)S(1)} copy-done((f32[5,3,1,64,128]{4,3,2,1,0:T(8,128)S(1)}, f32[5,3,1,64,128]{4,3,2,1,0:T(8,128)}, u32[]{:S(2)}) %copy-start) | copy-done | bytes 491544
  1.7 1.5 %pack.1 = bf16[4,8,3,16,128]{4,3,2,1,0:T(8,128)(2,1)} custom-call(f32[960,128]{1,0:T(8,128)S(1)} %bitcast.16), custom_call_target="tpu_custom_call" | custom-call | tf_op jit(solution)/shard_map/pack/pallas_call | solution.py:311
  3.2 0.0 copy-start.5
  3.2 0.0 copy-start.3
  3.2 0.0 copy-start.2
  3.2 7.3 %all-to-all-start = ((bf16[32,3,16,128]{3,2,1,0:T(8,128)(2,1)}), bf16[32,3,16,128]{3,2,1,0:T(8,128)(2,1)S(1)}, u32[]{:S(2)}, u32[]{:S(2)}) async-start(bf16[32,3,16,128]{3,2,1,0:T(8,128)(2,1)} %bitcast.1), calls=%async_computation | async-start | bytes 786432 | tf_op jit(solution)/shard_map/all_to_all | solution.py:309
  10.5 0.0 copy-done.5
  10.5 0.0 copy-start.4
  10.5 0.0 copy-done.3
  10.5 0.6 %copy-done.4 = s32[35]{0:T(128)S(1)} copy-done((s32[35]{0:T(128)S(1)}, s32[35]{0:T(128)}, u32[]{:S(2)}) %copy-start.4) | copy-done | bytes 164
  11.2 1.6 %prepare.1 = (bf16[40,1280]{1,0:T(8,128)(2,1)S(1)}, bf16[144,128]{1,0:T(8,128)(2,1)S(1)}, bf16[128,120]{1,0:T(8,128)(2,1)S(1)}, bf16[512,512]{1,0:T(8,128)(2,1)S(1)}) custom-call(s32[35]{0:T(128)S(1)} %copy-done.4, s32[3,4096]{1,0:T(4,128)S(1)} %bitcast.18, bf16[1,4096]{1,0:T(2,128)(2,1)S(1)} %reshape.34.coef_ref), custom_call_target="tpu_custom_call" | custom-call | tf_op jit(solution)/shard_map/prepare/pallas_call | solution.py:320
  12.8 10.9 %all-to-all-done = bf16[32,3,16,128]{3,2,1,0:T(8,128)(2,1)S(1)} async-done(((bf16[32,3,16,128]{3,2,1,0:T(8,128)(2,1)}), bf16[32,3,16,128]{3,2,1,0:T(8,128)(2,1)S(1)}, u32[]{:S(2)}, u32[]{:S(2)}) %all-to-all-start) | async-done | bytes 393248 | tf_op jit(solution)/shard_map/all_to_all | solution.py:309
  23.7 0.0 copy-done.2
  23.7 5.0 %contract.1 = bf16[4,8,2,16,128]{4,3,2,1,0:T(8,128)(2,1)S(1)} custom-call(bf16[4,8,3,16,128]{4,3,2,1,0:T(8,128)(2,1)S(1)} %bitcast.13, bf16[384,512]{1,0:T(8,128)(2,1)S(1)} %copy-done.2, bf16[40,1280]{1,0:T(8,128)(2,1)S(1)} %get-tuple-element.8.table_ref, bf16[144,128]{1,0:T(8,128)(2,1)S(1)} %get-tuple-element.9.pick_ref, ...), custom_call_target="tpu_custom_call" | custom-call | tf_op jit(solution)/shard_map/contract/pallas_call | solution.py:333
  28.6 0.0 copy-start.1
  28.6 13.0 %all_to_all.10 = bf16[32,2,16,128]{3,2,1,0:T(8,128)(2,1)S(1)} all-to-all(bf16[32,2,16,128]{3,2,1,0:T(8,128)(2,1)S(1)} %bitcast.14), channel_id=1, replica_groups=mesh['space'=4,'chaos'=8] {'space','chaos'}, dimensions={0} | all-to-all | bytes 524288 | tf_op jit(solution)/shard_map/all_to_all | solution.py:309
  41.7 0.0 copy-done.1
  41.7 1.5 %finish.1 = (f32[15,64,128]{2,1,0:T(8,128)}, f32[15,64,128]{2,1,0:T(8,128)}) custom-call(bf16[4,8,2,16,128]{4,3,2,1,0:T(8,128)(2,1)S(1)} %bitcast.15, f32[15,64,128]{2,1,0:T(8,128)S(1)} %bitcast.17, bf16[512,512]{1,0:T(8,128)(2,1)S(1)} %get-tuple-element.11.swap_ref), custom_call_target="tpu_custom_call" | custom-call | tf_op jit(solution)/shard_map/finish/pallas_call | solution.py:349
  (1 shorter events, 0.0 us)
Async XLA Ops:
  0.6 1.0 %copy-start = (f32[5,3,1,64,128]{4,3,2,1,0:T(8,128)S(1)}, f32[5,3,1,64,128]{4,3,2,1,0:T(8,128)}, u32[]{:S(2)}) copy-start(f32[5,3,1,64,128]{4,3,2,1,0:T(8,128)} %param.6) | copy-start | bytes 1474564
  3.2 7.3 %copy-start.5 = (bf16[4096]{0:T(1024)(128)(2,1)S(1)}, bf16[4096]{0:T(1024)(128)(2,1)}, u32[]{:S(2)}) copy-start(bf16[4096]{0:T(1024)(128)(2,1)} %param.10) | copy-start | bytes 24580
  3.2 7.4 %copy-start.3 = (s32[4096,3]{0,1:T(4,128)S(1)}, s32[4096,3]{0,1:T(4,128)}, u32[]{:S(2)}) copy-start(s32[4096,3]{0,1:T(4,128)} %param.9) | copy-start | bytes 147460
  3.2 20.5 %copy-start.2 = (bf16[384,512]{1,0:T(8,128)(2,1)S(1)}, bf16[384,512]{1,0:T(8,128)(2,1)}, u32[]{:S(2)}) copy-start(bf16[384,512]{1,0:T(8,128)(2,1)} %constant.2.clone.stencil_ref) | copy-start | bytes 1179652
  3.2 20.5 %all-to-all-start = ((bf16[32,3,16,128]{3,2,1,0:T(8,128)(2,1)}), bf16[32,3,16,128]{3,2,1,0:T(8,128)(2,1)S(1)}, u32[]{:S(2)}, u32[]{:S(2)}) async-start(bf16[32,3,16,128]{3,2,1,0:T(8,128)(2,1)} %bitcast.1), calls=%async_computation | async-start | bytes 786432 | tf_op jit(solution)/shard_map/all_to_all | solution.py:309
  10.5 0.7 %copy-start.4 = (s32[35]{0:T(128)S(1)}, s32[35]{0:T(128)}, u32[]{:S(2)}) copy-start(s32[35]{0:T(128)} %slot_ref.1) | copy-start | bytes 424
  28.6 13.0 %copy-start.1 = (f32[5,3,1,64,128]{4,3,2,1,0:T(8,128)S(1)}, f32[5,3,1,64,128]{4,3,2,1,0:T(8,128)}, u32[]{:S(2)}) copy-start(f32[5,3,1,64,128]{4,3,2,1,0:T(8,128)} %param.7) | copy-start | bytes 1474564
where the time goes:
time: 43.4 us; the launch traced here: 43.2 us
  blocking collectives  13 us (30%)
  waiting for transfers between devices  10.9 us (25%)
  Pallas kernels  9.6 us (22%)
  starting transfers between devices  7.3 us (17%)
  local copies, waits for them, and re-layouts  1.69 us (4%)
  between operations  0.7 us (2%)
    all_to_all x1, blocking collectives, exchange(): lax.all_to_all(flat, ('space', 'chaos'), 0, 0, tiled=True)  13 us
    all_to_all x1, waiting for transfers between devices, exchange(): lax.all_to_all(flat, ('space', 'chaos'), 0, 0, tiled=True)  10.9 us
    all_to_all x1, starting transfers between devices, exchange(): lax.all_to_all(flat, ('space', 'chaos'), 0, 0, tiled=True)  7.3 us
    pallas_call x1, Pallas kernels, on_device(): pl.pallas_call(functools.partial(contract_kernel, plan), out_shape=jax.Sh...  4.97 us
    unnamed x12, local copies, waits for them, and re-layouts  1.68 us
    pallas_call x1, Pallas kernels, on_device(): pl.pallas_call(functools.partial(prepare_kernel, plan), out_shape=[jax.Sh...  1.63 us
    pallas_call x1, Pallas kernels, on_device(): pl.pallas_call(functools.partial(pack_kernel, plan), out_shape=jax.ShapeD...  1.51 us
    pallas_call x1, Pallas kernels, on_device(): pl.pallas_call(functools.partial(finish_kernel, plan), out_shape=[jax.Sha...  1.5 us
  transfers between devices with their start and end apart: 1, of which 1 were waited for; matrix products, arithmetic and copies ran while one was open for 0% of the time, Pallas kernels for 4%

commit v1 on v0

--- a/solution.py
+++ b/solution.py
@@ -84,26 +84,34 @@
 
 
 def block_transposer(plan):
-    size = plan.planes * LANES
-    source = lax.broadcasted_iota(jnp.int32, (size, size), 0)
-    target = lax.broadcasted_iota(jnp.int32, (size, size), 1)
+    shape = (plan.planes * LANES, LANES)
+    source = lax.broadcasted_iota(jnp.int32, shape, 0)
+    target = lax.broadcasted_iota(jnp.int32, shape, 1)
     part, lane = source >> LANE_BITS, source & (LANES - 1)
     block, inner = lane >> plan.width_bits, lane & (plan.width - 1)
     wanted = (block << LANE_BITS) + (part << plan.width_bits) + inner
-    return jnp.where(target == wanted, 1.0, 0.0).astype(jnp.bfloat16)
+    return jnp.concatenate(
+        [jnp.where(wanted == target + b * LANES, 1.0, 0.0).astype(jnp.bfloat16) for b in range(plan.planes)], axis=1
+    )
 
 
 def side_collector(plan):
     source = lax.broadcasted_iota(jnp.int32, (plan.rows * LANES, LANES), 0)
-    target = lax.broadcasted_iota(jnp.int32, (plan.rows * LANES, LANES), 1)
+    target = lax.broadcasted_iota(jnp.int32, (1, LANES), 1)
     block, inner = target >> plan.width_bits, target & (plan.width - 1)
     beside = (block << plan.width_bits) - 1 + (inner & 1) * (plan.width + 1)
     wanted = ((inner >> 1) << LANE_BITS) + (beside & (LANES - 1))
-    return jnp.where((source == wanted) & (inner < 2 * plan.rows), 1.0, 0.0).astype(jnp.bfloat16)
-
-
-def pack_kernel(plan, v_ref, out_ref):
+    wanted = jnp.where(inner < 2 * plan.rows, wanted, -1)
+    return jnp.where(source == wanted, 1.0, 0.0).astype(jnp.bfloat16)
+
+
+def pack_kernel(plan, v_hbm, out_hbm, v_ref, out_ref, in_sem, out_sems):
     planes, rows, chunks, packed = plan.planes, plan.rows, plan.chunks, plan.packed
+    fetch = pltpu.make_async_copy(v_hbm, v_ref, in_sem)
+    fetch.start()
+    transposer = block_transposer(plan)
+    collector = side_collector(plan)
+    fetch.wait()
     pad = jnp.zeros((packed - plan.fields, LANES), jnp.float32)
     lines = []
     for y in range(plan.ny):
@@ -113,19 +121,23 @@
     def across(offset):
         return jnp.concatenate([lines[(c * rows + offset) % plan.ny] for c in range(chunks)], axis=0)
 
-    transposer = block_transposer(plan)
     inside = [across(r) for r in range(rows)]
-    side = jnp.dot(jnp.concatenate(inside, axis=1), side_collector(plan), preferred_element_type=jnp.float32)
+    side = jnp.dot(jnp.concatenate(inside, axis=1), collector, preferred_element_type=jnp.float32)
     blocks = inside + [jnp.zeros_like(inside[0])] * (plan.vectors * planes - rows)
     blocks[plan.low] = across(-1)
     blocks[plan.high] = across(rows)
     blocks[plan.side] = side.astype(jnp.bfloat16)
+    copies = []
     for v in range(plan.vectors):
         row = jnp.concatenate(blocks[v * planes : (v + 1) * planes], axis=1)
         swapped = jnp.dot(row, transposer, preferred_element_type=jnp.float32).astype(jnp.bfloat16)
         for s in range(planes):
             for c in range(chunks):
                 out_ref[s, c, v] = swapped[c * packed : (c + 1) * packed, s * LANES : (s + 1) * LANES]
+        copies.append(pltpu.make_async_copy(out_ref.at[:, :, v], out_hbm.at[:, :, v], out_sems.at[v]))
+        copies[-1].start()
+    for copy in copies:
+        copy.wait()
 
 
 def prepare_kernel(plan, slot_ref, triples_ref, coef_ref, table_ref, pick_ref, place_ref, swap_ref):
@@ -175,7 +187,8 @@
 
 
 def contract_kernel(plan, got_ref, stencil_ref, table_ref, pick_ref, place_ref, out_ref, *scratch):
-    moving_ref, row_ref, slope_ref, conv_ref, even_ref, odd_ref = scratch
+    conv_ref, even_ref, odd_ref = scratch[:3]
+    even_fields, odd_fields = scratch[3:6], scratch[6:9]
     planes, inner, pad, main, wide = plan.planes, plan.inner, plan.mode_pad, plan.main, plan.wide_pad
     tail = plan.pairs + plan.rest_rows
     if tail < plan.depth:
@@ -183,23 +196,24 @@
             ref[tail:, :] = jnp.zeros((plan.depth - tail, ref.shape[1]), jnp.bfloat16)
 
     def vector(p, v):
-        return got_ref[p % planes, :, v].reshape(plan.wide, LANES)
-
-    for p in range(planes):
+        return got_ref[lax.rem(p, planes), :, v].reshape(plan.wide, LANES)
+
+    def prepare(fields, p):
+        moving_ref, row_ref, slope_ref = fields
         center = jnp.concatenate([vector(p, v) for v in range(plan.vectors)], axis=1)
-        along_x = [
-            (0.5 * (vector(p + 1, v).astype(jnp.float32) - vector(p - 1, v).astype(jnp.float32))).astype(jnp.bfloat16)
-            for v in range(inner)
-        ]
+        along_x = []
+        for v in range(inner):
+            ahead, behind = vector(p + 1, v), vector(p + planes - 1, v)
+            along_x.append((0.5 * (ahead.astype(jnp.float32) - behind.astype(jnp.float32))).astype(jnp.bfloat16))
         along_yz = jnp.dot(center, stencil_ref[...], preferred_element_type=jnp.float32).astype(jnp.bfloat16)
         moving = center[:, : inner * LANES]
-        moving_ref[p] = jnp.dot(pick_ref[...], moving, preferred_element_type=jnp.float32)
+        moving_ref[...] = jnp.dot(pick_ref[...], moving, preferred_element_type=jnp.float32)
         slopes = jnp.dot(
             pick_ref[...], jnp.concatenate(along_x + [along_yz], axis=1), preferred_element_type=jnp.float32
         )
-        slope_ref[p] = slopes.astype(jnp.bfloat16)
+        slope_ref[...] = slopes.astype(jnp.bfloat16)
         for c in range(COMPS):
-            row_ref[p, c * 8 : (c + 1) * 8] = slopes[c * wide + main : c * wide + main + 8]
+            row_ref[c * 8 : (c + 1) * 8] = slopes[c * wide + main : c * wide + main + 8]
 
     def repeated(row):
         return jnp.broadcast_to(row, (PACK, LANES)).astype(jnp.bfloat16)
@@ -210,7 +224,8 @@
             term = term + left[d] * right[d]
         return term
 
-    def fill(prod_ref, p, v):
+    def fill(prod_ref, fields, v):
+        moving_ref, row_ref, slope_ref = fields
         here = slice(v * LANES, (v + 1) * LANES)
 
         def there(d):
@@ -220,23 +235,23 @@
             return slice((v * COMPS + c) * LANES, (v * COMPS + c + 1) * LANES)
 
         slopes = {
-            (c, j): [slope_ref[p, c * wide + j : c * wide + j + PACK, there(d)] for d in range(COMPS)]
+            (c, j): [slope_ref[c * wide + j : c * wide + j + PACK, there(d)] for d in range(COMPS)]
             for c in range(COMPS)
             for j in range(0, main, PACK)
         }
         for i in range(plan.modes):
-            moving = [repeated(moving_ref[p, d * wide + i : d * wide + i + 1, here]) for d in range(COMPS)]
+            moving = [repeated(moving_ref[d * wide + i : d * wide + i + 1, here]) for d in range(COMPS)]
             for c in range(COMPS):
                 for j in range(0, main, PACK):
                     prod_ref[i * main + j : i * main + j + PACK, lanes(c)] = along(moving, slopes[c, j])
         if plan.rest:
             moving = {
-                i: [moving_ref[p, d * wide + i : d * wide + i + PACK, here].astype(jnp.bfloat16) for d in range(COMPS)]
+                i: [moving_ref[d * wide + i : d * wide + i + PACK, here].astype(jnp.bfloat16) for d in range(COMPS)]
                 for i in range(0, wide, PACK)
             }
             for c in range(COMPS):
                 for j in range(plan.rest):
-                    slope = [repeated(row_ref[p, c * 8 + j : c * 8 + j + 1, there(d)]) for d in range(COMPS)]
+                    slope = [repeated(row_ref[c * 8 + j : c * 8 + j + 1, there(d)]) for d in range(COMPS)]
                     for i in range(0, wide, PACK):
                         at = plan.pairs + j * wide + i
                         prod_ref[at : at + PACK, lanes(c)] = along(moving[i], slope)
@@ -248,21 +263,24 @@
             v, c = divmod(at // LANES, COMPS)
             conv_ref[slot, v, c * pad : (c + 1) * pad, :] = result[:, at - low : at - low + LANES]
 
-    def beside(prod_ref, p, done_ref, slot):
+    def beside(prod_ref, fields, done_ref, slot):
         cuts = list(plan.cuts)
         for v in range(inner):
             if cuts:
                 multiply(slot, done_ref, cuts.pop(0))
-            fill(prod_ref, p, v)
+            fill(prod_ref, fields, v)
         for cut in cuts:
             multiply(slot, done_ref, cut)
 
     def two_planes(step, carry):
         p = 2 * step
-        beside(even_ref, p, odd_ref, p)
-        beside(odd_ref, p + 1, even_ref, p + 1)
+        prepare(odd_fields, p + 1)
+        beside(even_ref, even_fields, odd_ref, p)
+        prepare(even_fields, p + 2)
+        beside(odd_ref, odd_fields, even_ref, p + 1)
         return carry
 
+    prepare(even_fields, 0)
     lax.fori_loop(0, planes // 2, two_planes, 0)
     for cut in plan.cuts:
         multiply(planes, odd_ref, cut)
@@ -311,8 +329,14 @@
     sent = pl.pallas_call(
         functools.partial(pack_kernel, plan),
         out_shape=jax.ShapeDtypeStruct((planes, chunks, plan.vectors, packed, LANES), jnp.bfloat16),
-        in_specs=[vmem_spec()],
-        out_specs=vmem_spec(),
+        in_specs=[pl.BlockSpec(memory_space=pl.ANY)],
+        out_specs=pl.BlockSpec(memory_space=pl.ANY),
+        scratch_shapes=[
+            pltpu.VMEM((fields * ny, nz), jnp.float32),
+            pltpu.VMEM((planes, chunks, plan.vectors, packed, LANES), jnp.bfloat16),
+            pltpu.SemaphoreType.DMA,
+            pltpu.SemaphoreType.DMA((plan.vectors,)),
+        ],
         compiler_params=params(),
         name="pack",
     )(velocity.reshape(fields * ny, nz))
@@ -336,13 +360,16 @@
         in_specs=[vmem_spec()] * 5,
         out_specs=vmem_spec(),
         scratch_shapes=[
-            pltpu.VMEM((planes, COMPS * plan.wide_pad, plan.inner * LANES), jnp.float32),
-            pltpu.VMEM((planes, COMPS * 8, plan.lanes), jnp.float32),
-            pltpu.VMEM((planes, COMPS * plan.wide_pad, plan.lanes), jnp.bfloat16),
             pltpu.VMEM((planes + 1, plan.inner, COMPS * plan.mode_pad, LANES), jnp.float32),
             pltpu.VMEM((plan.depth, plan.lanes), jnp.bfloat16),
             pltpu.VMEM((plan.depth, plan.lanes), jnp.bfloat16),
-        ],
+        ]
+        + [
+            pltpu.VMEM((COMPS * plan.wide_pad, plan.inner * LANES), jnp.float32),
+            pltpu.VMEM((COMPS * 8, plan.lanes), jnp.float32),
+            pltpu.VMEM((COMPS * plan.wide_pad, plan.lanes), jnp.bfloat16),
+        ]
+        * 2,
         compiler_params=params(),
         name="contract",
     )(got, jnp.asarray(plan.stencil(), jnp.bfloat16), table, pick, place)

time: 43.4 us -> 43.9 us (1.012)
  no operation moved by 1% of the time
where the time goes in v1:
time: 43.9 us; the launch traced here: 43.6 us
  blocking collectives  13 us (30%)
  waiting for transfers between devices  10.9 us (25%)
  Pallas kernels  10 us (23%)
  starting transfers between devices  7.3 us (17%)
  local copies, waits for them, and re-layouts  1.7 us (4%)
  between operations  0.73 us (2%)
    all_to_all x1, blocking collectives, exchange(): lax.all_to_all(flat, ('space', 'chaos'), 0, 0, tiled=True)  13 us
    all_to_all x1, waiting for transfers between devices, exchange(): lax.all_to_all(flat, ('space', 'chaos'), 0, 0, tiled=True)  10.9 us
    all_to_all x1, starting transfers between devices, exchange(): lax.all_to_all(flat, ('space', 'chaos'), 0, 0, tiled=True)  7.3 us
    pallas_call x1, Pallas kernels, on_device(): pl.pallas_call(functools.partial(contract_kernel, plan), out_shape=jax.Sh...  4.96 us
    pallas_call x1, Pallas kernels, on_device(): pl.pallas_call(functools.partial(pack_kernel, plan), out_shape=jax.ShapeD...  1.92 us
    unnamed x12, local copies, waits for them, and re-layouts  1.69 us
    pallas_call x1, Pallas kernels, on_device(): pl.pallas_call(functools.partial(prepare_kernel, plan), out_shape=[jax.Sh...  1.63 us
    pallas_call x1, Pallas kernels, on_device(): pl.pallas_call(functools.partial(finish_kernel, plan), out_shape=[jax.Sha...  1.5 us
  transfers between devices with their start and end apart: 1, of which 1 were waited for; matrix products, arithmetic and copies ran while one was open for 0% of the time, Pallas kernels for 4%

profile of v1, /device:TPU:0, one launch (start us, length us, event | category | flops | bytes accessed | tf_op | source)
XLA Modules:
  0.0 43.6 jit_solution(5185988832773965303)
XLA Ops:
  0.6 0.0 copy-start
  0.6 1.0 %copy-done = f32[5,3,1,64,128]{4,3,2,1,0:T(8,128)S(1)} copy-done((f32[5,3,1,64,128]{4,3,2,1,0:T(8,128)S(1)}, f32[5,3,1,64,128]{4,3,2,1,0:T(8,128)}, u32[]{:S(2)}) %copy-start) | copy-done | bytes 491544
  1.7 1.9 %pack.1 = bf16[4,8,3,16,128]{4,3,2,1,0:T(8,128)(2,1)} custom-call(f32[960,128]{1,0:T(8,128)S(1)} %bitcast.16), custom_call_target="tpu_custom_call" | custom-call | tf_op jit(solution)/shard_map/pack/pallas_call | solution.py:329
  3.6 0.0 copy-start.5
  3.6 0.0 copy-start.3
  3.6 0.0 copy-start.2
  3.6 7.3 %all-to-all-start = ((bf16[32,3,16,128]{3,2,1,0:T(8,128)(2,1)}), bf16[32,3,16,128]{3,2,1,0:T(8,128)(2,1)S(1)}, u32[]{:S(2)}, u32[]{:S(2)}) async-start(bf16[32,3,16,128]{3,2,1,0:T(8,128)(2,1)} %bitcast.1), calls=%async_computation | async-start | bytes 786432 | tf_op jit(solution)/shard_map/all_to_all | solution.py:327
  10.9 0.0 copy-done.5
  11.0 0.0 copy-start.4
  11.0 0.0 copy-done.3
  11.0 0.6 %copy-done.4 = s32[35]{0:T(128)S(1)} copy-done((s32[35]{0:T(128)S(1)}, s32[35]{0:T(128)}, u32[]{:S(2)}) %copy-start.4) | copy-done | bytes 164
  11.6 1.6 %prepare.1 = (bf16[40,1280]{1,0:T(8,128)(2,1)S(1)}, bf16[144,128]{1,0:T(8,128)(2,1)S(1)}, bf16[128,120]{1,0:T(8,128)(2,1)S(1)}, bf16[512,512]{1,0:T(8,128)(2,1)S(1)}) custom-call(s32[35]{0:T(128)S(1)} %copy-done.4, s32[3,4096]{1,0:T(4,128)S(1)} %bitcast.18, bf16[1,4096]{1,0:T(2,128)(2,1)S(1)} %reshape.34.coef_ref), custom_call_target="tpu_custom_call" | custom-call | tf_op jit(solution)/shard_map/prepare/pallas_call | solution.py:344
  13.3 10.9 %all-to-all-done = bf16[32,3,16,128]{3,2,1,0:T(8,128)(2,1)S(1)} async-done(((bf16[32,3,16,128]{3,2,1,0:T(8,128)(2,1)}), bf16[32,3,16,128]{3,2,1,0:T(8,128)(2,1)S(1)}, u32[]{:S(2)}, u32[]{:S(2)}) %all-to-all-start) | async-done | bytes 393248 | tf_op jit(solution)/shard_map/all_to_all | solution.py:327
  24.1 0.0 copy-done.2
  24.1 5.0 %contract.1 = bf16[4,8,2,16,128]{4,3,2,1,0:T(8,128)(2,1)S(1)} custom-call(bf16[4,8,3,16,128]{4,3,2,1,0:T(8,128)(2,1)S(1)} %bitcast.13, bf16[384,512]{1,0:T(8,128)(2,1)S(1)} %copy-done.2, bf16[40,1280]{1,0:T(8,128)(2,1)S(1)} %get-tuple-element.8.table_ref, bf16[144,128]{1,0:T(8,128)(2,1)S(1)} %get-tuple-element.9.pick_ref, ...), custom_call_target="tpu_custom_call" | custom-call | tf_op jit(solution)/shard_map/contract/pallas_call | solution.py:357
  29.1 0.0 copy-start.1
  29.1 13.0 %all_to_all.10 = bf16[32,2,16,128]{3,2,1,0:T(8,128)(2,1)S(1)} all-to-all(bf16[32,2,16,128]{3,2,1,0:T(8,128)(2,1)S(1)} %bitcast.14), channel_id=1, replica_groups=mesh['space'=4,'chaos'=8] {'space','chaos'}, dimensions={0} | all-to-all | bytes 524288 | tf_op jit(solution)/shard_map/all_to_all | solution.py:327
  42.1 0.0 copy-done.1
  42.1 1.5 %finish.1 = (f32[15,64,128]{2,1,0:T(8,128)}, f32[15,64,128]{2,1,0:T(8,128)}) custom-call(bf16[4,8,2,16,128]{4,3,2,1,0:T(8,128)(2,1)S(1)} %bitcast.15, f32[15,64,128]{2,1,0:T(8,128)S(1)} %bitcast.17, bf16[512,512]{1,0:T(8,128)(2,1)S(1)} %get-tuple-element.11.swap_ref), custom_call_target="tpu_custom_call" | custom-call | tf_op jit(solution)/shard_map/finish/pallas_call | solution.py:376
  (1 shorter events, 0.0 us)
Async XLA Ops:
  0.6 1.0 %copy-start = (f32[5,3,1,64,128]{4,3,2,1,0:T(8,128)S(1)}, f32[5,3,1,64,128]{4,3,2,1,0:T(8,128)}, u32[]{:S(2)}) copy-start(f32[5,3,1,64,128]{4,3,2,1,0:T(8,128)} %param.6) | copy-start | bytes 1474564
  3.6 7.4 %copy-start.5 = (bf16[4096]{0:T(1024)(128)(2,1)S(1)}, bf16[4096]{0:T(1024)(128)(2,1)}, u32[]{:S(2)}) copy-start(bf16[4096]{0:T(1024)(128)(2,1)} %param.10) | copy-start | bytes 24580
  3.6 7.4 %copy-start.3 = (s32[4096,3]{0,1:T(4,128)S(1)}, s32[4096,3]{0,1:T(4,128)}, u32[]{:S(2)}) copy-start(s32[4096,3]{0,1:T(4,128)} %param.9) | copy-start | bytes 147460
  3.6 20.5 %copy-start.2 = (bf16[384,512]{1,0:T(8,128)(2,1)S(1)}, bf16[384,512]{1,0:T(8,128)(2,1)}, u32[]{:S(2)}) copy-start(bf16[384,512]{1,0:T(8,128)(2,1)} %constant.2.clone.stencil_ref) | copy-start | bytes 1179652
  3.6 20.5 %all-to-all-start = ((bf16[32,3,16,128]{3,2,1,0:T(8,128)(2,1)}), bf16[32,3,16,128]{3,2,1,0:T(8,128)(2,1)S(1)}, u32[]{:S(2)}, u32[]{:S(2)}) async-start(bf16[32,3,16,128]{3,2,1,0:T(8,128)(2,1)} %bitcast.1), calls=%async_computation | async-start | bytes 786432 | tf_op jit(solution)/shard_map/all_to_all | solution.py:327
  11.0 0.7 %copy-start.4 = (s32[35]{0:T(128)S(1)}, s32[35]{0:T(128)}, u32[]{:S(2)}) copy-start(s32[35]{0:T(128)} %slot_ref.1) | copy-start | bytes 424
  29.1 13.1 %copy-start.1 = (f32[5,3,1,64,128]{4,3,2,1,0:T(8,128)S(1)}, f32[5,3,1,64,128]{4,3,2,1,0:T(8,128)}, u32[]{:S(2)}) copy-start(f32[5,3,1,64,128]{4,3,2,1,0:T(8,128)} %param.7) | copy-start | bytes 1474564

commit v2 on v1

--- a/solution.py
+++ b/solution.py
@@ -15,6 +15,7 @@
 TILE = 256
 PACK = 16
 VMEM_LIMIT = 48 * 1024 * 1024
+PACK_VMEM_LIMIT = 65280 * 1024
 
 
 def round_up(value, unit):
@@ -25,8 +26,8 @@
     return pl.BlockSpec(memory_space=pltpu.VMEM)
 
 
-def params():
-    return pltpu.CompilerParams(vmem_limit_bytes=VMEM_LIMIT)
+def params(limit=VMEM_LIMIT):
+    return pltpu.CompilerParams(vmem_limit_bytes=limit)
 
 
 class Plan:
@@ -187,30 +188,32 @@
 
 
 def contract_kernel(plan, got_ref, stencil_ref, table_ref, pick_ref, place_ref, out_ref, *scratch):
-    conv_ref, even_ref, odd_ref = scratch[:3]
-    even_fields, odd_fields = scratch[3:6], scratch[6:9]
+    conv_ref, beside_ref = scratch[:2]
+    prod_refs, field_refs = scratch[2:4], (scratch[4:7], scratch[7:10])
     planes, inner, pad, main, wide = plan.planes, plan.inner, plan.mode_pad, plan.main, plan.wide_pad
     tail = plan.pairs + plan.rest_rows
     if tail < plan.depth:
-        for ref in (even_ref, odd_ref):
+        for ref in prod_refs:
             ref[tail:, :] = jnp.zeros((plan.depth - tail, ref.shape[1]), jnp.bfloat16)
 
     def vector(p, v):
-        return got_ref[lax.rem(p, planes), :, v].reshape(plan.wide, LANES)
+        return got_ref[p % planes, :, v].reshape(plan.wide, LANES)
+
+    centers = [jnp.concatenate([vector(p, v) for v in range(plan.vectors)], axis=1) for p in range(planes)]
+    beside_ref[...] = jnp.dot(
+        jnp.concatenate(centers, axis=0), stencil_ref[...], preferred_element_type=jnp.float32
+    ).astype(jnp.bfloat16)
 
     def prepare(fields, p):
         moving_ref, row_ref, slope_ref = fields
-        center = jnp.concatenate([vector(p, v) for v in range(plan.vectors)], axis=1)
-        along_x = []
+        parts = [vector(p, v) for v in range(inner)]
         for v in range(inner):
-            ahead, behind = vector(p + 1, v), vector(p + planes - 1, v)
-            along_x.append((0.5 * (ahead.astype(jnp.float32) - behind.astype(jnp.float32))).astype(jnp.bfloat16))
-        along_yz = jnp.dot(center, stencil_ref[...], preferred_element_type=jnp.float32).astype(jnp.bfloat16)
-        moving = center[:, : inner * LANES]
-        moving_ref[...] = jnp.dot(pick_ref[...], moving, preferred_element_type=jnp.float32)
-        slopes = jnp.dot(
-            pick_ref[...], jnp.concatenate(along_x + [along_yz], axis=1), preferred_element_type=jnp.float32
-        )
+            ahead, behind = vector(p + 1, v), vector(p - 1, v)
+            parts.append((0.5 * (ahead.astype(jnp.float32) - behind.astype(jnp.float32))).astype(jnp.bfloat16))
+        parts.append(beside_ref[p * plan.wide : (p + 1) * plan.wide, :])
+        picked = jnp.dot(pick_ref[...], jnp.concatenate(parts, axis=1), preferred_element_type=jnp.float32)
+        moving_ref[...] = picked[:, : inner * LANES]
+        slopes = picked[:, inner * LANES :]
         slope_ref[...] = slopes.astype(jnp.bfloat16)
         for c in range(COMPS):
             row_ref[c * 8 : (c + 1) * 8] = slopes[c * wide + main : c * wide + main + 8]
@@ -263,29 +266,21 @@
             v, c = divmod(at // LANES, COMPS)
             conv_ref[slot, v, c * pad : (c + 1) * pad, :] = result[:, at - low : at - low + LANES]
 
-    def beside(prod_ref, fields, done_ref, slot):
-        cuts = list(plan.cuts)
+    prepare(field_refs[0], 0)
+    for p in range(planes):
+        cuts = list(plan.cuts) if p else []
+        if p + 1 < planes:
+            prepare(field_refs[(p + 1) % 2], p + 1)
         for v in range(inner):
             if cuts:
-                multiply(slot, done_ref, cuts.pop(0))
-            fill(prod_ref, fields, v)
+                multiply(p - 1, prod_refs[(p - 1) % 2], cuts.pop(0))
+            fill(prod_refs[p % 2], field_refs[p % 2], v)
         for cut in cuts:
-            multiply(slot, done_ref, cut)
-
-    def two_planes(step, carry):
-        p = 2 * step
-        prepare(odd_fields, p + 1)
-        beside(even_ref, even_fields, odd_ref, p)
-        prepare(even_fields, p + 2)
-        beside(odd_ref, odd_fields, even_ref, p + 1)
-        return carry
-
-    prepare(even_fields, 0)
-    lax.fori_loop(0, planes // 2, two_planes, 0)
+            multiply(p - 1, prod_refs[(p - 1) % 2], cut)
     for cut in plan.cuts:
-        multiply(planes, odd_ref, cut)
+        multiply(planes - 1, prod_refs[(planes - 1) % 2], cut)
     for p in range(planes):
-        stacked = jnp.concatenate([conv_ref[p + 1, v].astype(jnp.bfloat16) for v in range(inner)], axis=1)
+        stacked = jnp.concatenate([conv_ref[p, v].astype(jnp.bfloat16) for v in range(inner)], axis=1)
         placed = jnp.dot(place_ref[...], stacked, preferred_element_type=jnp.float32).astype(jnp.bfloat16)
         for v in range(inner):
             block = placed[:, v * LANES : (v + 1) * LANES]
@@ -329,15 +324,15 @@
     sent = pl.pallas_call(
         functools.partial(pack_kernel, plan),
         out_shape=jax.ShapeDtypeStruct((planes, chunks, plan.vectors, packed, LANES), jnp.bfloat16),
-        in_specs=[pl.BlockSpec(memory_space=pl.ANY)],
-        out_specs=pl.BlockSpec(memory_space=pl.ANY),
+        in_specs=[pl.BlockSpec(memory_space=pltpu.HBM)],
+        out_specs=pl.BlockSpec(memory_space=pltpu.HBM),
         scratch_shapes=[
             pltpu.VMEM((fields * ny, nz), jnp.float32),
             pltpu.VMEM((planes, chunks, plan.vectors, packed, LANES), jnp.bfloat16),
             pltpu.SemaphoreType.DMA,
             pltpu.SemaphoreType.DMA((plan.vectors,)),
         ],
-        compiler_params=params(),
+        compiler_params=params(PACK_VMEM_LIMIT),
         name="pack",
     )(velocity.reshape(fields * ny, nz))
     got = exchange(sent)
@@ -360,7 +355,8 @@
         in_specs=[vmem_spec()] * 5,
         out_specs=vmem_spec(),
         scratch_shapes=[
-            pltpu.VMEM((planes + 1, plan.inner, COMPS * plan.mode_pad, LANES), jnp.float32),
+            pltpu.VMEM((planes, plan.inner, COMPS * plan.mode_pad, LANES), jnp.float32),
+            pltpu.VMEM((planes * plan.wide, 2 * plan.inner * LANES), jnp.bfloat16),
             pltpu.VMEM((plan.depth, plan.lanes), jnp.bfloat16),
             pltpu.VMEM((plan.depth, plan.lanes), jnp.bfloat16),
         ]

time: 43.9 us -> 42.7 us (0.973)
  local copies, waits for them, and re-layouts: 1.7 us -> 0.68 us
    unnamed x12 -> x10, local copies, waits for them, and re-layouts: 1.69 us -> 0.67 us
    pallas_call x1, Pallas kernels: 4.96 us -> 4.33 us  [on_device(): pl.pallas_call(functools.partial(contract_kernel, plan), out_shape=jax.Sh...]
    pallas_call x1, Pallas kernels: 1.92 us -> 2.37 us  [on_device(): pl.pallas_call(functools.partial(pack_kernel, plan), out_shape=jax.ShapeD...]
where the time goes in v2:
time: 42.7 us; the launch traced here: 42.4 us
  blocking collectives  13 us (30%)
  waiting for transfers between devices  10.8 us (25%)
  Pallas kernels  9.83 us (23%)
  starting transfers between devices  7.3 us (17%)
  between operations  0.72 us (2%)
  local copies, waits for them, and re-layouts  0.68 us (2%)
    all_to_all x1, blocking collectives, exchange(): lax.all_to_all(flat, ('space', 'chaos'), 0, 0, tiled=True)  13 us
    all_to_all x1, waiting for transfers between devices, exchange(): lax.all_to_all(flat, ('space', 'chaos'), 0, 0, tiled=True)  10.8 us
    all_to_all x1, starting transfers between devices, exchange(): lax.all_to_all(flat, ('space', 'chaos'), 0, 0, tiled=True)  7.3 us
    pallas_call x1, Pallas kernels, on_device(): pl.pallas_call(functools.partial(contract_kernel, plan), out_shape=jax.Sh...  4.33 us
    pallas_call x1, Pallas kernels, on_device(): pl.pallas_call(functools.partial(pack_kernel, plan), out_shape=jax.ShapeD...  2.37 us
    pallas_call x1, Pallas kernels, on_device(): pl.pallas_call(functools.partial(prepare_kernel, plan), out_shape=[jax.Sh...  1.63 us
    pallas_call x1, Pallas kernels, on_device(): pl.pallas_call(functools.partial(finish_kernel, plan), out_shape=[jax.Sha...  1.5 us
  transfers between devices with their start and end apart: 1, of which 1 were waited for; matrix products, arithmetic and copies ran while one was open for 0% of the time, Pallas kernels for 4%

profile of v2, /device:TPU:0, one launch (start us, length us, event | category | flops | bytes accessed | tf_op | source)
XLA Modules:
  0.0 42.4 jit_solution(7056230104208764830)
XLA Ops:
  0.6 2.4 %pack.1 = bf16[4,8,3,16,128]{4,3,2,1,0:T(8,128)(2,1)} custom-call(f32[960,128]{1,0:T(8,128)} %bitcast.19), custom_call_target="tpu_custom_call" | custom-call | tf_op jit(solution)/shard_map/pack/pallas_call | solution.py:324
  3.0 0.0 copy-start.4
  3.0 0.0 copy-start.2
  3.0 0.0 copy-start.1
  3.0 7.3 %all-to-all-start = ((bf16[32,3,16,128]{3,2,1,0:T(8,128)(2,1)}), bf16[32,3,16,128]{3,2,1,0:T(8,128)(2,1)S(1)}, u32[]{:S(2)}, u32[]{:S(2)}) async-start(bf16[32,3,16,128]{3,2,1,0:T(8,128)(2,1)} %bitcast.18), calls=%async_computation | async-start | bytes 786432 | tf_op jit(solution)/shard_map/all_to_all | solution.py:322
  10.4 0.0 copy-done.4
  10.4 0.0 copy-start.3
  10.4 0.0 copy-done.2
  10.4 0.6 %copy-done.3 = s32[35]{0:T(128)S(1)} copy-done((s32[35]{0:T(128)S(1)}, s32[35]{0:T(128)}, u32[]{:S(2)}) %copy-start.3) | copy-done | bytes 164
  11.0 1.6 %prepare.1 = (bf16[40,1280]{1,0:T(8,128)(2,1)S(1)}, bf16[144,128]{1,0:T(8,128)(2,1)S(1)}, bf16[128,120]{1,0:T(8,128)(2,1)S(1)}, bf16[512,512]{1,0:T(8,128)(2,1)S(1)}) custom-call(s32[35]{0:T(128)S(1)} %copy-done.3, s32[3,4096]{1,0:T(4,128)S(1)} %bitcast.17, bf16[1,4096]{1,0:T(2,128)(2,1)S(1)} %reshape.34.coef_ref), custom_call_target="tpu_custom_call" | custom-call | tf_op jit(solution)/shard_map/prepare/pallas_call | solution.py:339
  12.7 10.8 %all-to-all-done = bf16[32,3,16,128]{3,2,1,0:T(8,128)(2,1)S(1)} async-done(((bf16[32,3,16,128]{3,2,1,0:T(8,128)(2,1)}), bf16[32,3,16,128]{3,2,1,0:T(8,128)(2,1)S(1)}, u32[]{:S(2)}, u32[]{:S(2)}) %all-to-all-start) | async-done | bytes 393248 | tf_op jit(solution)/shard_map/all_to_all | solution.py:322
  23.5 0.0 copy-done.1
  23.5 4.3 %contract.1 = bf16[4,8,2,16,128]{4,3,2,1,0:T(8,128)(2,1)S(1)} custom-call(bf16[4,8,3,16,128]{4,3,2,1,0:T(8,128)(2,1)S(1)} %bitcast.13, bf16[384,512]{1,0:T(8,128)(2,1)S(1)} %copy-done.1, bf16[40,1280]{1,0:T(8,128)(2,1)S(1)} %get-tuple-element.8.table_ref, bf16[144,128]{1,0:T(8,128)(2,1)S(1)} %get-tuple-element.9.pick_ref, ...), custom_call_target="tpu_custom_call" | custom-call | tf_op jit(solution)/shard_map/contract/pallas_call | solution.py:352
  27.9 0.0 copy-start
  27.9 13.0 %all_to_all.10 = bf16[32,2,16,128]{3,2,1,0:T(8,128)(2,1)S(1)} all-to-all(bf16[32,2,16,128]{3,2,1,0:T(8,128)(2,1)S(1)} %bitcast.14), channel_id=1, replica_groups=mesh['space'=4,'chaos'=8] {'space','chaos'}, dimensions={0} | all-to-all | bytes 524288 | tf_op jit(solution)/shard_map/all_to_all | solution.py:322
  40.9 0.0 copy-done
  40.9 1.5 %finish.1 = (f32[15,64,128]{2,1,0:T(8,128)}, f32[15,64,128]{2,1,0:T(8,128)}) custom-call(bf16[4,8,2,16,128]{4,3,2,1,0:T(8,128)(2,1)S(1)} %bitcast.15, f32[15,64,128]{2,1,0:T(8,128)S(1)} %bitcast.16, bf16[512,512]{1,0:T(8,128)(2,1)S(1)} %get-tuple-element.11.swap_ref), custom_call_target="tpu_custom_call" | custom-call | tf_op jit(solution)/shard_map/finish/pallas_call | solution.py:372
  (1 shorter events, 0.0 us)
Async XLA Ops:
  3.0 7.4 %copy-start.4 = (bf16[4096]{0:T(1024)(128)(2,1)S(1)}, bf16[4096]{0:T(1024)(128)(2,1)}, u32[]{:S(2)}) copy-start(bf16[4096]{0:T(1024)(128)(2,1)} %param.10) | copy-start | bytes 24580
  3.0 7.4 %copy-start.2 = (s32[4096,3]{0,1:T(4,128)S(1)}, s32[4096,3]{0,1:T(4,128)}, u32[]{:S(2)}) copy-start(s32[4096,3]{0,1:T(4,128)} %param.9) | copy-start | bytes 147460
  3.0 20.5 %copy-start.1 = (bf16[384,512]{1,0:T(8,128)(2,1)S(1)}, bf16[384,512]{1,0:T(8,128)(2,1)}, u32[]{:S(2)}) copy-start(bf16[384,512]{1,0:T(8,128)(2,1)} %constant.2.clone.stencil_ref) | copy-start | bytes 1179652
  3.0 20.5 %all-to-all-start = ((bf16[32,3,16,128]{3,2,1,0:T(8,128)(2,1)}), bf16[32,3,16,128]{3,2,1,0:T(8,128)(2,1)S(1)}, u32[]{:S(2)}, u32[]{:S(2)}) async-start(bf16[32,3,16,128]{3,2,1,0:T(8,128)(2,1)} %bitcast.18), calls=%async_computation | async-start | bytes 786432 | tf_op jit(solution)/shard_map/all_to_all | solution.py:322
  10.4 0.7 %copy-start.3 = (s32[35]{0:T(128)S(1)}, s32[35]{0:T(128)}, u32[]{:S(2)}) copy-start(s32[35]{0:T(128)} %slot_ref.1) | copy-start | bytes 424
  27.9 13.1 %copy-start = (f32[5,3,1,64,128]{4,3,2,1,0:T(8,128)S(1)}, f32[5,3,1,64,128]{4,3,2,1,0:T(8,128)}, u32[]{:S(2)}) copy-start(f32[5,3,1,64,128]{4,3,2,1,0:T(8,128)} %param.7) | copy-start | bytes 1474564

commit v3 on v2

--- a/solution.py
+++ b/solution.py
@@ -129,14 +129,20 @@
     blocks[plan.high] = across(rows)
     blocks[plan.side] = side.astype(jnp.bfloat16)
     copies = []
-    for v in range(plan.vectors):
-        row = jnp.concatenate(blocks[v * planes : (v + 1) * planes], axis=1)
+    for part in (range(plan.inner), range(plan.inner, plan.vectors)):
+        if not part:
+            continue
+        row = jnp.concatenate(
+            [jnp.concatenate(blocks[v * planes : (v + 1) * planes], axis=1) for v in part], axis=0
+        )
         swapped = jnp.dot(row, transposer, preferred_element_type=jnp.float32).astype(jnp.bfloat16)
-        for s in range(planes):
-            for c in range(chunks):
-                out_ref[s, c, v] = swapped[c * packed : (c + 1) * packed, s * LANES : (s + 1) * LANES]
-        copies.append(pltpu.make_async_copy(out_ref.at[:, :, v], out_hbm.at[:, :, v], out_sems.at[v]))
-        copies[-1].start()
+        for at, v in enumerate(part):
+            for s in range(planes):
+                for c in range(chunks):
+                    first = at * plan.wide + c * packed
+                    out_ref[s, c, v] = swapped[first : first + packed, s * LANES : (s + 1) * LANES]
+            copies.append(pltpu.make_async_copy(out_ref.at[:, :, v], out_hbm.at[:, :, v], out_sems.at[v]))
+            copies[-1].start()
     for copy in copies:
         copy.wait()
 
@@ -267,18 +273,18 @@
             conv_ref[slot, v, c * pad : (c + 1) * pad, :] = result[:, at - low : at - low + LANES]
 
     prepare(field_refs[0], 0)
+    ready = []
     for p in range(planes):
-        cuts = list(plan.cuts) if p else []
         if p + 1 < planes:
             prepare(field_refs[(p + 1) % 2], p + 1)
         for v in range(inner):
-            if cuts:
-                multiply(p - 1, prod_refs[(p - 1) % 2], cuts.pop(0))
+            while ready:
+                multiply(*ready.pop(0))
             fill(prod_refs[p % 2], field_refs[p % 2], v)
-        for cut in cuts:
-            multiply(p - 1, prod_refs[(p - 1) % 2], cut)
-    for cut in plan.cuts:
-        multiply(planes - 1, prod_refs[(planes - 1) % 2], cut)
+            done, filled = v * COMPS * LANES, (v + 1) * COMPS * LANES
+            ready = [(p, prod_refs[p % 2], cut) for cut in plan.cuts if done < cut[1] <= filled]
+    while ready:
+        multiply(*ready.pop(0))
     for p in range(planes):
         stacked = jnp.concatenate([conv_ref[p, v].astype(jnp.bfloat16) for v in range(inner)], axis=1)
         placed = jnp.dot(place_ref[...], stacked, preferred_element_type=jnp.float32).astype(jnp.bfloat16)
@@ -288,14 +294,18 @@
 
 
 def finish_kernel(plan, got_ref, base_ref, swap_ref, conv_ref, next_ref, flat_ref, conv_vmem, next_vmem, sems):
+    rows = [
+        jnp.concatenate([got_ref[s, :, v].reshape(plan.wide, LANES) for s in range(plan.planes)], axis=1)
+        for v in range(plan.inner)
+    ]
+    swapped = jnp.dot(jnp.concatenate(rows, axis=0), swap_ref[...], preferred_element_type=jnp.float32)
     for v in range(plan.inner):
-        parts = [got_ref[s, :, v].reshape(plan.wide, LANES) for s in range(plan.planes)]
-        swapped = jnp.dot(jnp.concatenate(parts, axis=1), swap_ref[...], preferred_element_type=jnp.float32)
         for block in range(min(plan.planes, plan.rows - v * plan.planes)):
             for chunk in range(plan.chunks):
                 at = (chunk * plan.rows + v * plan.planes + block) * plan.packed
+                first = v * plan.wide + chunk * plan.packed
                 flat_ref[at : at + plan.packed, :] = swapped[
-                    chunk * plan.packed : (chunk + 1) * plan.packed, block * LANES : (block + 1) * LANES
+                    first : first + plan.packed, block * LANES : (block + 1) * LANES
                 ]
     copies = []
     for s in range(plan.slot_dev):

time: 42.7 us -> 42.2 us (0.988)
  Pallas kernels: 9.83 us -> 9.39 us
    pallas_call x1, Pallas kernels: 4.33 us -> 3.9 us  [on_device(): pl.pallas_call(functools.partial(contract_kernel, plan), out_shape=jax.Sh...]
where the time goes in v3:
time: 42.2 us; the launch traced here: 42 us
  blocking collectives  13 us (31%)
  waiting for transfers between devices  10.8 us (26%)
  Pallas kernels  9.39 us (22%)
  starting transfers between devices  7.3 us (17%)
  between operations  0.72 us (2%)
  local copies, waits for them, and re-layouts  0.68 us (2%)
    all_to_all x1, blocking collectives, exchange(): lax.all_to_all(flat, ('space', 'chaos'), 0, 0, tiled=True)  13 us
    all_to_all x1, waiting for transfers between devices, exchange(): lax.all_to_all(flat, ('space', 'chaos'), 0, 0, tiled=True)  10.8 us
    all_to_all x1, starting transfers between devices, exchange(): lax.all_to_all(flat, ('space', 'chaos'), 0, 0, tiled=True)  7.3 us
    pallas_call x1, Pallas kernels, on_device(): pl.pallas_call(functools.partial(contract_kernel, plan), out_shape=jax.Sh...  3.9 us
    pallas_call x1, Pallas kernels, on_device(): pl.pallas_call(functools.partial(pack_kernel, plan), out_shape=jax.ShapeD...  2.36 us
    pallas_call x1, Pallas kernels, on_device(): pl.pallas_call(functools.partial(prepare_kernel, plan), out_shape=[jax.Sh...  1.63 us
    pallas_call x1, Pallas kernels, on_device(): pl.pallas_call(functools.partial(finish_kernel, plan), out_shape=[jax.Sha...  1.49 us
  transfers between devices with their start and end apart: 1, of which 1 were waited for; matrix products, arithmetic and copies ran while one was open for 0% of the time, Pallas kernels for 4%

profile of v3, /device:TPU:0, one launch (start us, length us, event | category | flops | bytes accessed | tf_op | source)
XLA Modules:
  0.0 42.0 jit_solution(15401121307078240326)
XLA Ops:
  0.6 2.4 %pack.1 = bf16[4,8,3,16,128]{4,3,2,1,0:T(8,128)(2,1)} custom-call(f32[960,128]{1,0:T(8,128)} %bitcast.19), custom_call_target="tpu_custom_call" | custom-call | tf_op jit(solution)/shard_map/pack/pallas_call | solution.py:334
  3.0 0.0 copy-start.4
  3.0 0.0 copy-start.2
  3.0 0.0 copy-start.1
  3.0 7.3 %all-to-all-start = ((bf16[32,3,16,128]{3,2,1,0:T(8,128)(2,1)}), bf16[32,3,16,128]{3,2,1,0:T(8,128)(2,1)S(1)}, u32[]{:S(2)}, u32[]{:S(2)}) async-start(bf16[32,3,16,128]{3,2,1,0:T(8,128)(2,1)} %bitcast.18), calls=%async_computation | async-start | bytes 786432 | tf_op jit(solution)/shard_map/all_to_all | solution.py:332
  10.3 0.0 copy-done.4
  10.4 0.0 copy-start.3
  10.4 0.0 copy-done.2
  10.4 0.6 %copy-done.3 = s32[35]{0:T(128)S(1)} copy-done((s32[35]{0:T(128)S(1)}, s32[35]{0:T(128)}, u32[]{:S(2)}) %copy-start.3) | copy-done | bytes 164
  11.0 1.6 %prepare.1 = (bf16[40,1280]{1,0:T(8,128)(2,1)S(1)}, bf16[144,128]{1,0:T(8,128)(2,1)S(1)}, bf16[128,120]{1,0:T(8,128)(2,1)S(1)}, bf16[512,512]{1,0:T(8,128)(2,1)S(1)}) custom-call(s32[35]{0:T(128)S(1)} %copy-done.3, s32[3,4096]{1,0:T(4,128)S(1)} %bitcast.17, bf16[1,4096]{1,0:T(2,128)(2,1)S(1)} %reshape.34.coef_ref), custom_call_target="tpu_custom_call" | custom-call | tf_op jit(solution)/shard_map/prepare/pallas_call | solution.py:349
  12.7 10.8 %all-to-all-done = bf16[32,3,16,128]{3,2,1,0:T(8,128)(2,1)S(1)} async-done(((bf16[32,3,16,128]{3,2,1,0:T(8,128)(2,1)}), bf16[32,3,16,128]{3,2,1,0:T(8,128)(2,1)S(1)}, u32[]{:S(2)}, u32[]{:S(2)}) %all-to-all-start) | async-done | bytes 393248 | tf_op jit(solution)/shard_map/all_to_all | solution.py:332
  23.5 0.0 copy-done.1
  23.5 3.9 %contract.1 = bf16[4,8,2,16,128]{4,3,2,1,0:T(8,128)(2,1)S(1)} custom-call(bf16[4,8,3,16,128]{4,3,2,1,0:T(8,128)(2,1)S(1)} %bitcast.13, bf16[384,512]{1,0:T(8,128)(2,1)S(1)} %copy-done.1, bf16[40,1280]{1,0:T(8,128)(2,1)S(1)} %get-tuple-element.8.table_ref, bf16[144,128]{1,0:T(8,128)(2,1)S(1)} %get-tuple-element.9.pick_ref, ...), custom_call_target="tpu_custom_call" | custom-call | tf_op jit(solution)/shard_map/contract/pallas_call | solution.py:362
  27.4 0.0 copy-start
  27.5 13.0 %all_to_all.10 = bf16[32,2,16,128]{3,2,1,0:T(8,128)(2,1)S(1)} all-to-all(bf16[32,2,16,128]{3,2,1,0:T(8,128)(2,1)S(1)} %bitcast.14), channel_id=1, replica_groups=mesh['space'=4,'chaos'=8] {'space','chaos'}, dimensions={0} | all-to-all | bytes 524288 | tf_op jit(solution)/shard_map/all_to_all | solution.py:332
  40.5 0.0 copy-done
  40.5 1.5 %finish.1 = (f32[15,64,128]{2,1,0:T(8,128)}, f32[15,64,128]{2,1,0:T(8,128)}) custom-call(bf16[4,8,2,16,128]{4,3,2,1,0:T(8,128)(2,1)S(1)} %bitcast.15, f32[15,64,128]{2,1,0:T(8,128)S(1)} %bitcast.16, bf16[512,512]{1,0:T(8,128)(2,1)S(1)} %get-tuple-element.11.swap_ref), custom_call_target="tpu_custom_call" | custom-call | tf_op jit(solution)/shard_map/finish/pallas_call | solution.py:382
  (1 shorter events, 0.0 us)
Async XLA Ops:
  3.0 7.3 %copy-start.4 = (bf16[4096]{0:T(1024)(128)(2,1)S(1)}, bf16[4096]{0:T(1024)(128)(2,1)}, u32[]{:S(2)}) copy-start(bf16[4096]{0:T(1024)(128)(2,1)} %param.10) | copy-start | bytes 24580
  3.0 7.4 %copy-start.2 = (s32[4096,3]{0,1:T(4,128)S(1)}, s32[4096,3]{0,1:T(4,128)}, u32[]{:S(2)}) copy-start(s32[4096,3]{0,1:T(4,128)} %param.9) | copy-start | bytes 147460
  3.0 20.5 %copy-start.1 = (bf16[384,512]{1,0:T(8,128)(2,1)S(1)}, bf16[384,512]{1,0:T(8,128)(2,1)}, u32[]{:S(2)}) copy-start(bf16[384,512]{1,0:T(8,128)(2,1)} %constant.2.clone.stencil_ref) | copy-start | bytes 1179652
  3.0 20.5 %all-to-all-start = ((bf16[32,3,16,128]{3,2,1,0:T(8,128)(2,1)}), bf16[32,3,16,128]{3,2,1,0:T(8,128)(2,1)S(1)}, u32[]{:S(2)}, u32[]{:S(2)}) async-start(bf16[32,3,16,128]{3,2,1,0:T(8,128)(2,1)} %bitcast.18), calls=%async_computation | async-start | bytes 786432 | tf_op jit(solution)/shard_map/all_to_all | solution.py:332
  10.4 0.7 %copy-start.3 = (s32[35]{0:T(128)S(1)}, s32[35]{0:T(128)}, u32[]{:S(2)}) copy-start(s32[35]{0:T(128)} %slot_ref.1) | copy-start | bytes 424
  27.4 13.1 %copy-start = (f32[5,3,1,64,128]{4,3,2,1,0:T(8,128)S(1)}, f32[5,3,1,64,128]{4,3,2,1,0:T(8,128)}, u32[]{:S(2)}) copy-start(f32[5,3,1,64,128]{4,3,2,1,0:T(8,128)} %param.7) | copy-start | bytes 1474564

commit v4 on v3

--- a/solution.py
+++ b/solution.py
@@ -206,9 +206,11 @@
         return got_ref[p % planes, :, v].reshape(plan.wide, LANES)
 
     centers = [jnp.concatenate([vector(p, v) for v in range(plan.vectors)], axis=1) for p in range(planes)]
-    beside_ref[...] = jnp.dot(
-        jnp.concatenate(centers, axis=0), stencil_ref[...], preferred_element_type=jnp.float32
-    ).astype(jnp.bfloat16)
+
+    def slope_beside(first, last):
+        row = jnp.concatenate(centers[first:last], axis=0)
+        slopes = jnp.dot(row, stencil_ref[...], preferred_element_type=jnp.float32)
+        beside_ref[first * plan.wide : last * plan.wide, :] = slopes.astype(jnp.bfloat16)
 
     def prepare(fields, p):
         moving_ref, row_ref, slope_ref = fields
@@ -272,7 +274,9 @@
             v, c = divmod(at // LANES, COMPS)
             conv_ref[slot, v, c * pad : (c + 1) * pad, :] = result[:, at - low : at - low + LANES]
 
+    slope_beside(0, 1)
     prepare(field_refs[0], 0)
+    slope_beside(1, planes)
     ready = []
     for p in range(planes):
         if p + 1 < planes:

time: 42.2 us -> 42.2 us (level)
  no operation moved by 1% of the time
where the time goes in v4:
time: 42.2 us; the launch traced here: 42 us
  blocking collectives  13 us (31%)
  waiting for transfers between devices  10.8 us (26%)
  Pallas kernels  9.39 us (22%)
  starting transfers between devices  7.3 us (17%)
  between operations  0.72 us (2%)
  local copies, waits for them, and re-layouts  0.68 us (2%)
    all_to_all x1, blocking collectives, exchange(): lax.all_to_all(flat, ('space', 'chaos'), 0, 0, tiled=True)  13 us
    all_to_all x1, waiting for transfers between devices, exchange(): lax.all_to_all(flat, ('space', 'chaos'), 0, 0, tiled=True)  10.8 us
    all_to_all x1, starting transfers between devices, exchange(): lax.all_to_all(flat, ('space', 'chaos'), 0, 0, tiled=True)  7.3 us
    pallas_call x1, Pallas kernels, on_device(): pl.pallas_call(functools.partial(contract_kernel, plan), out_shape=jax.Sh...  3.91 us
    pallas_call x1, Pallas kernels, on_device(): pl.pallas_call(functools.partial(pack_kernel, plan), out_shape=jax.ShapeD...  2.36 us
    pallas_call x1, Pallas kernels, on_device(): pl.pallas_call(functools.partial(prepare_kernel, plan), out_shape=[jax.Sh...  1.63 us
    pallas_call x1, Pallas kernels, on_device(): pl.pallas_call(functools.partial(finish_kernel, plan), out_shape=[jax.Sha...  1.49 us
  transfers between devices with their start and end apart: 1, of which 1 were waited for; matrix products, arithmetic and copies ran while one was open for 0% of the time, Pallas kernels for 4%

profile of v4, /device:TPU:0, one launch (start us, length us, event | category | flops | bytes accessed | tf_op | source)
XLA Modules:
  0.0 42.0 jit_solution(3607557712408688208)
XLA Ops:
  0.6 2.4 %pack.1 = bf16[4,8,3,16,128]{4,3,2,1,0:T(8,128)(2,1)} custom-call(f32[960,128]{1,0:T(8,128)} %bitcast.19), custom_call_target="tpu_custom_call" | custom-call | tf_op jit(solution)/shard_map/pack/pallas_call | solution.py:338
  3.0 0.0 copy-start.4
  3.0 0.0 copy-start.2
  3.0 0.0 copy-start.1
  3.0 7.3 %all-to-all-start = ((bf16[32,3,16,128]{3,2,1,0:T(8,128)(2,1)}), bf16[32,3,16,128]{3,2,1,0:T(8,128)(2,1)S(1)}, u32[]{:S(2)}, u32[]{:S(2)}) async-start(bf16[32,3,16,128]{3,2,1,0:T(8,128)(2,1)} %bitcast.18), calls=%async_computation | async-start | bytes 786432 | tf_op jit(solution)/shard_map/all_to_all | solution.py:336
  10.3 0.0 copy-done.4
  10.4 0.0 copy-start.3
  10.4 0.0 copy-done.2
  10.4 0.6 %copy-done.3 = s32[35]{0:T(128)S(1)} copy-done((s32[35]{0:T(128)S(1)}, s32[35]{0:T(128)}, u32[]{:S(2)}) %copy-start.3) | copy-done | bytes 164
  11.0 1.6 %prepare.1 = (bf16[40,1280]{1,0:T(8,128)(2,1)S(1)}, bf16[144,128]{1,0:T(8,128)(2,1)S(1)}, bf16[128,120]{1,0:T(8,128)(2,1)S(1)}, bf16[512,512]{1,0:T(8,128)(2,1)S(1)}) custom-call(s32[35]{0:T(128)S(1)} %copy-done.3, s32[3,4096]{1,0:T(4,128)S(1)} %bitcast.17, bf16[1,4096]{1,0:T(2,128)(2,1)S(1)} %reshape.34.coef_ref), custom_call_target="tpu_custom_call" | custom-call | tf_op jit(solution)/shard_map/prepare/pallas_call | solution.py:353
  12.7 10.8 %all-to-all-done = bf16[32,3,16,128]{3,2,1,0:T(8,128)(2,1)S(1)} async-done(((bf16[32,3,16,128]{3,2,1,0:T(8,128)(2,1)}), bf16[32,3,16,128]{3,2,1,0:T(8,128)(2,1)S(1)}, u32[]{:S(2)}, u32[]{:S(2)}) %all-to-all-start) | async-done | bytes 393248 | tf_op jit(solution)/shard_map/all_to_all | solution.py:336
  23.5 0.0 copy-done.1
  23.5 3.9 %contract.1 = bf16[4,8,2,16,128]{4,3,2,1,0:T(8,128)(2,1)S(1)} custom-call(bf16[4,8,3,16,128]{4,3,2,1,0:T(8,128)(2,1)S(1)} %bitcast.13, bf16[384,512]{1,0:T(8,128)(2,1)S(1)} %copy-done.1, bf16[40,1280]{1,0:T(8,128)(2,1)S(1)} %get-tuple-element.8.table_ref, bf16[144,128]{1,0:T(8,128)(2,1)S(1)} %get-tuple-element.9.pick_ref, ...), custom_call_target="tpu_custom_call" | custom-call | tf_op jit(solution)/shard_map/contract/pallas_call | solution.py:366
  27.4 0.0 copy-start
  27.5 13.0 %all_to_all.10 = bf16[32,2,16,128]{3,2,1,0:T(8,128)(2,1)S(1)} all-to-all(bf16[32,2,16,128]{3,2,1,0:T(8,128)(2,1)S(1)} %bitcast.14), channel_id=1, replica_groups=mesh['space'=4,'chaos'=8] {'space','chaos'}, dimensions={0} | all-to-all | bytes 524288 | tf_op jit(solution)/shard_map/all_to_all | solution.py:336
  40.5 0.0 copy-done
  40.5 1.5 %finish.1 = (f32[15,64,128]{2,1,0:T(8,128)}, f32[15,64,128]{2,1,0:T(8,128)}) custom-call(bf16[4,8,2,16,128]{4,3,2,1,0:T(8,128)(2,1)S(1)} %bitcast.15, f32[15,64,128]{2,1,0:T(8,128)S(1)} %bitcast.16, bf16[512,512]{1,0:T(8,128)(2,1)S(1)} %get-tuple-element.11.swap_ref), custom_call_target="tpu_custom_call" | custom-call | tf_op jit(solution)/shard_map/finish/pallas_call | solution.py:386
  (1 shorter events, 0.0 us)
Async XLA Ops:
  3.0 7.3 %copy-start.4 = (bf16[4096]{0:T(1024)(128)(2,1)S(1)}, bf16[4096]{0:T(1024)(128)(2,1)}, u32[]{:S(2)}) copy-start(bf16[4096]{0:T(1024)(128)(2,1)} %param.10) | copy-start | bytes 24580
  3.0 7.4 %copy-start.2 = (s32[4096,3]{0,1:T(4,128)S(1)}, s32[4096,3]{0,1:T(4,128)}, u32[]{:S(2)}) copy-start(s32[4096,3]{0,1:T(4,128)} %param.9) | copy-start | bytes 147460
  3.0 20.5 %copy-start.1 = (bf16[384,512]{1,0:T(8,128)(2,1)S(1)}, bf16[384,512]{1,0:T(8,128)(2,1)}, u32[]{:S(2)}) copy-start(bf16[384,512]{1,0:T(8,128)(2,1)} %constant.2.clone.stencil_ref) | copy-start | bytes 1179652
  3.0 20.5 %all-to-all-start = ((bf16[32,3,16,128]{3,2,1,0:T(8,128)(2,1)}), bf16[32,3,16,128]{3,2,1,0:T(8,128)(2,1)S(1)}, u32[]{:S(2)}, u32[]{:S(2)}) async-start(bf16[32,3,16,128]{3,2,1,0:T(8,128)(2,1)} %bitcast.18), calls=%async_computation | async-start | bytes 786432 | tf_op jit(solution)/shard_map/all_to_all | solution.py:336
  10.4 0.7 %copy-start.3 = (s32[35]{0:T(128)S(1)}, s32[35]{0:T(128)}, u32[]{:S(2)}) copy-start(s32[35]{0:T(128)} %slot_ref.1) | copy-start | bytes 424
  27.4 13.1 %copy-start = (f32[5,3,1,64,128]{4,3,2,1,0:T(8,128)S(1)}, f32[5,3,1,64,128]{4,3,2,1,0:T(8,128)}, u32[]{:S(2)}) copy-start(f32[5,3,1,64,128]{4,3,2,1,0:T(8,128)} %param.7) | copy-start | bytes 1474564
